TPU v7x, 32 devices: a whole 2x2x4 slice. The times are simulated.
32 devices in a mesh: groups: 2 (over x), atom: 16 (over z, y, core).
Axes of the slice: x: 2, y: 2, z: 4, core: 2. Of those that a mesh axis runs over, the one named last changes fastest.
Arguments:
- atoms: float32 [128, 4096], P('atom'), may hold values from 0.2 to 2
- images: float32 [32, 16384], P(('groups', 'atom')), parts along dimension 0, may hold values from 0.2 to 2
- logits: float32 [32, 32], P(('groups', 'atom')), parts along dimension 0, may hold values from -4 to 4
Outputs:
- barycenters: float32 [32, 16384], P(('groups', 'atom')), parts along dimension 0
- atom_gradient: float32 [256, 4096], P(('groups', 'atom')), parts along dimension 0
There are 2 independent parts, one for each index of `groups`. A program takes and returns all parts, laid end to end along the dimension named above; an argument that names none is the same for every part. Nothing has to cross between parts.
All inputs are finite; a program needn't handle non-finite values.
Results may differ from a plain program's by a relative error of at most 0.0001.
Values sent between devices are 32-bit elements; how exact they have to be, the bound alone decides.
A program may use at most 64 MiB of HBM per device.

v0:
```python
import functools

import jax
import jax.numpy as jnp
import numpy as np
from jax import lax
from jax.experimental import pallas as pl
from jax.experimental.pallas import tpu as pltpu
from jax.sharding import PartitionSpec as P

K = 32
HALF = 15
SPREAD = 50.0
SLAB = 4

f32 = jnp.float32
bf16 = jnp.bfloat16


def split(x):
    hi = x.astype(bf16)
    lo = (x - hi.astype(f32)).astype(bf16)
    return hi, lo


def kernel_matrix(count):
    taps = np.arange(-HALF, HALF + 1, dtype=np.float64)
    total = float(np.sum(np.exp(-taps * taps / SPREAD)))
    i = lax.broadcasted_iota(jnp.int32, (count, count), 0)
    j = lax.broadcasted_iota(jnp.int32, (count, count), 1)
    d = (i - j).astype(f32)
    return jnp.where(jnp.abs(d) <= HALF, jnp.exp(d * d * (-1.0 / SPREAD)), 0.0) * (1.0 / total)


def kernel(H, W, a_ref, y_ref, logit_ref, p_ref, da_ref,
           wc, wr, re_ref, lam, rq1, rq2, rq3, rb2, rb3, u, p1, p2, acc, usum):
    gc = kernel_matrix(W)
    gr = kernel_matrix(H)
    ch, cl = split(gc)
    rh, rl = split(gr)
    wc[:W, :W] = ch
    wc[W:, :W] = ch
    wc[:W, W:] = cl
    wc[W:, W:] = jnp.zeros_like(cl)
    wr[:H, :H] = rh
    wr[:H, H:] = rh
    wr[H:, :H] = rl
    wr[H:, H:] = jnp.zeros_like(rl)
    re_ref[...] = 1.0 / (jnp.sum(gr, axis=1, keepdims=True) * jnp.sum(gc, axis=0, keepdims=True))
    e = jnp.exp(logit_ref[...])
    soft = e / jnp.sum(e, axis=1, keepdims=True)
    for k in range(K):
        lam[:, k * W:(k + 1) * W] = jnp.broadcast_to(soft[:, k:k + 1], (1, W))

    def blur(fields):
        left = []
        for x in fields:
            hi, lo = split(x)
            left.append(jnp.concatenate([hi, lo], axis=1))
        out = jnp.dot(jnp.concatenate(left, axis=0), wc[...], preferred_element_type=f32)
        out = out[:, :W] + out[:, W:]
        right = []
        for n in range(len(fields)):
            hi, lo = split(out[n * H:(n + 1) * H])
            right.append(jnp.concatenate([hi, lo], axis=0))
        out = jnp.dot(wr[...], jnp.concatenate(right, axis=1), preferred_element_type=f32)
        out = out[:H] + out[H:]
        return [out[:, n * W:(n + 1) * W] for n in range(len(fields))]

    def over_slabs(step):
        def one(s, carry):
            step([pl.ds(pl.multiple_of((s * SLAB + n) * W, W), W) for n in range(SLAB)])
            return carry
        lax.fori_loop(0, K // SLAB, one, 0)

    def add(total, parts):
        s = parts[0]
        for x in parts[1:]:
            s = s + x
        total[...] += s

    acc[...] = jnp.zeros_like(acc)

    def first(cols):
        q = blur([a_ref[:, c] * re_ref[...] for c in cols])
        for c, x in zip(cols, q):
            rq1[:, c] = 1.0 / x
        add(acc, [lam[:, c] * jnp.log(x) for c, x in zip(cols, q)])
    over_slabs(first)

    def forward(p, rq_in, rb, rq_out):
        p[...] = jnp.exp(acc[...])
        acc[...] = jnp.zeros_like(acc)

        def step(cols):
            b = blur([p[...] * rq_in[:, c] for c in cols])
            r = []
            for c, x in zip(cols, b):
                inv = 1.0 / x
                rb[:, c] = inv
                r.append(a_ref[:, c] * inv)
            q = blur(r)
            for c, x in zip(cols, q):
                rq_out[:, c] = 1.0 / x
            add(acc, [lam[:, c] * jnp.log(x) for c, x in zip(cols, q)])
        over_slabs(step)

    forward(p1, rq1, rb2, rq2)
    forward(p2, rq2, rb3, rq3)
    result = jnp.exp(acc[...])
    p_ref[...] = result
    acc[...] = (y_ref[...] - result) * result

    def backward(p, rq, rb, rq_before, newest):
        usum[...] = acc[...]
        acc[...] = jnp.zeros_like(acc)

        def step(cols):
            dq = []
            for c in cols:
                g = lam[:, c] * usum[...]
                g = -g if newest else u[:, c] - g
                dq.append(g * rq[:, c])
            dr = blur(dq)
            db = []
            for c, x in zip(cols, dr):
                inv = rb[:, c]
                t = x * inv
                if newest:
                    da_ref[:, c] = t
                else:
                    da_ref[:, c] += t
                db.append(t * (a_ref[:, c] * inv))
            dv = blur(db)
            parts = []
            for c, x in zip(cols, dv):
                x = x * (p[...] * rq_before[:, c])
                u[:, c] = x
                parts.append(x)
            add(acc, parts)
        over_slabs(step)

    backward(p2, rq3, rb3, rq2, True)
    backward(p1, rq2, rb2, rq1, False)
    usum[...] = acc[...]

    def last(cols):
        d = blur([(u[:, c] - lam[:, c] * usum[...]) * rq1[:, c] for c in cols])
        for c, x in zip(cols, d):
            da_ref[:, c] += x * re_ref[...]
    over_slabs(last)


def body(atoms, images, logits, *, parts):
    rows, wide = atoms.shape
    H, W = rows * parts, wide // K
    gathered = lax.all_gather(atoms, "atom", axis=0, tiled=True)
    field = pltpu.VMEM((H, wide), f32)
    plane = pltpu.VMEM((H, W), f32)
    call = pl.pallas_call(
        functools.partial(kernel, H, W),
        out_shape=(jax.ShapeDtypeStruct((H, W), f32), jax.ShapeDtypeStruct((H, wide), f32)),
        in_specs=[pl.BlockSpec(memory_space=pltpu.VMEM)] * 3,
        out_specs=[pl.BlockSpec(memory_space=pltpu.VMEM)] * 2,
        scratch_shapes=[
            pltpu.VMEM((2 * W, 2 * W), bf16),
            pltpu.VMEM((2 * H, 2 * H), bf16),
            plane,
            pltpu.VMEM((1, wide), f32),
            field, field, field, field, field, field,
            plane, plane, plane, plane,
        ],
        compiler_params=pltpu.CompilerParams(vmem_limit_bytes=40 * 2**20),
    )
    results, grads = [], []
    for n in range(images.shape[0]):
        p, da = call(gathered, images[n].reshape(H, W), logits[n:n + 1])
        results.append(p.reshape(1, H * W))
        grads.append(da)
    result = results[0] if len(results) == 1 else jnp.concatenate(results, axis=0)
    term = sum(grads[1:], grads[0])
    return result, lax.psum_scatter(term, "atom", scatter_dimension=0, tiled=True)


def solution(mesh):
    return jax.shard_map(
        functools.partial(body, parts=mesh.shape["atom"]),
        mesh=mesh,
        in_specs=(P("atom", None), P(("groups", "atom"), None), P(("groups", "atom"), None)),
        out_specs=(P(("groups", "atom"), None), P(("groups", "atom"), None)),
        check_vma=False,
    )
```

profile of v0, /device:TPU:0, one launch (start us, length us, event | category | flops | bytes accessed | tf_op | source)
XLA Modules:
  0.0 162.2 jit_solution(12931393589319729553)
XLA Ops:
  7.2 0.0 all-gather.2.cloned.1.call-start
  7.2 0.7 all-gather.2.cloned.1.call-update
  7.9 0.0 reduce-scatter.2.cloned.1.call-start
  7.9 46.3 %all-gather.2.cloned.1.call-done.a_ref = f32[128,4096]{1,0:T(8,128)} async-done(((f32[8,4096]{1,0:T(8,128)}), f32[128,4096]{1,0:T(8,128)}) %all-gather.2.cloned.1.call-update) | async-done | bytes 2097168 | tf_op jit(solution)/shard_map/all_gather | solution.py:157
  54.3 0.0 copy-start
  54.3 1.6 copy-done
  55.9 0.0 copy-start.1
  55.9 0.8 copy-done.1
  56.7 0.0 copy-start.2
  56.7 0.7 copy-done.2
  57.4 37.5 %shard_map.50 = (f32[128,128]{1,0:T(8,128)}, f32[128,4096]{1,0:T(8,128)}) custom-call(f32[128,4096]{1,0:T(8,128)S(1)} %copy-done, f32[128,128]{1,0:T(8,128)S(1)} %bitcast.2, f32[1,32]{1,0:T(1,128)S(1)} %copy-done.2), custom_call_target="tpu_custom_call" | custom-call | tf_op jit(solution)/shard_map/pallas_call | solution.py:177
  94.8 0.0 reduce-scatter.2.cloned.1.call-update
  94.9 60.5 %reduce-scatter.2.cloned.1.call-done = f32[8,4096]{1,0:T(8,128)} async-done(((f32[128,4096]{1,0:T(8,128)}), f32[8,4096]{1,0:T(8,128)}) %reduce-scatter.2.cloned.1.call-update) | async-done | bytes 131088 | tf_op jit(solution)/shard_map/reduce_scatter | solution.py:182
Async XLA Ops:
  7.2 47.1 %all-gather.2.cloned.1.call-start = ((), (), s32[]{:S(2)}) async-start(), calls=%async_computation.1 | async-start | bytes 2228224 | tf_op jit(solution)/shard_map/all_gather | solution.py:157
  7.9 147.5 %reduce-scatter.2.cloned.1.call-start = ((), (), s32[]{:S(2)}) async-start(), calls=%async_computation.2 | async-start | bytes 2228224 | tf_op jit(solution)/shard_map/reduce_scatter | solution.py:182
  54.3 1.6 copy-start
  55.9 0.8 copy-start.1
  56.7 0.7 copy-start.2
Sparse Core Ops, SparseCore 0:
  10.2 44.0 all-gather.1
  95.0 60.3 reduce-scatter.1
where the time goes:
time: 162 us
  waiting for transfers between devices  108 us (67%)
  Pallas kernels  37.5 us (23%)
  between operations  14 us (9%)
  local copies, waits for them, and re-layouts  3.08 us (2%)
    reduce_scatter x1, waiting for transfers between devices, body(): lax.psum_scatter(term, 'atom', scatter_dimension=0, tiled=True)  60.5 us
    all_gather x1, waiting for transfers between devices, body(): gathered = lax.all_gather(atoms, 'atom', axis=0, tiled=True)  46.3 us
    pallas_call x1, Pallas kernels, body(): p, da = call(gathered, images[n].reshape(H, W), logits[n:n + 1])  37.5 us
  transfers between devices with their start and end apart: 2, of which 2 were waited for; matrix products, arithmetic and copies ran while one was open for 0% of the time, Pallas kernels for 0%

commit v1 on v0

--- a/solution.py
+++ b/solution.py
@@ -12,6 +12,7 @@
 HALF = 15
 SPREAD = 50.0
 SLAB = 4
+CHUNKS = 4
 
 f32 = jnp.float32
 bf16 = jnp.bfloat16
@@ -32,8 +33,186 @@
     return jnp.where(jnp.abs(d) <= HALF, jnp.exp(d * d * (-1.0 / SPREAD)), 0.0) * (1.0 / total)
 
 
-def kernel(H, W, a_ref, y_ref, logit_ref, p_ref, da_ref,
-           wc, wr, re_ref, lam, rq1, rq2, rq3, rb2, rb3, u, p1, p2, acc, usum):
+def chip_grid(parts):
+    chips = parts // 2
+    ny = 2 ** ((chips.bit_length() - 1) // 2)
+    return chips // ny, ny
+
+
+class Links:
+    def __init__(self, parts, rows, x_ref, out_ref, a_ref, da_ref, rc, sy, ry, keep, sz, rz, sems):
+        self.nz, self.ny = chip_grid(parts)
+        self.rows = rows
+        self.x_ref, self.out_ref, self.a_ref, self.da_ref = x_ref, out_ref, a_ref, da_ref
+        self.rc, self.sy, self.ry, self.keep, self.sz, self.rz = rc, sy, ry, keep, sz, rz
+        self.sems = sems
+        me = lax.axis_index("atom")
+        self.me = me
+        self.c = lax.rem(me, 2)
+        self.y = lax.rem(me // 2, self.ny)
+        self.z = me // (2 * self.ny)
+        self.width = a_ref.shape[1] // CHUNKS
+        self.sent = []
+        self.live = {}
+
+    def index(self, z, y, c):
+        return (z * self.ny + y) * 2 + c
+
+    def zp(self, d):
+        return lax.rem(self.z + d, self.nz)
+
+    def zm(self, d):
+        return lax.rem(self.z + self.nz - d, self.nz)
+
+    def yp(self, d):
+        return lax.rem(self.y + d, self.ny)
+
+    def ym(self, d):
+        return lax.rem(self.y + self.ny - d, self.ny)
+
+    def barrier(self):
+        bar = pltpu.get_barrier_semaphore()
+        peers = [self.index(self.z, self.y, 1 - self.c)]
+        peers += [self.index(self.zp(d), self.y, self.c) for d in range(1, self.nz)]
+        peers += [self.index(self.z, self.yp(d), self.c) for d in range(1, self.ny)]
+        for peer in peers:
+            pl.semaphore_signal(bar, inc=1, device_id={"atom": peer}, device_id_type=pl.DeviceIdType.MESH)
+        pl.semaphore_wait(bar, len(peers))
+
+    def send(self, key, number, src, dst, peer):
+        send, recv = self.sems
+        copy = pltpu.make_async_remote_copy(
+            src_ref=src, dst_ref=dst, send_sem=send.at[number], recv_sem=recv.at[number],
+            device_id={"atom": peer}, device_id_type=pl.DeviceIdType.MESH)
+        copy.start()
+        self.live[key] = copy
+        self.sent.append(copy)
+
+    def arrived(self, key):
+        self.live[key].wait_recv()
+
+    def finish(self):
+        for copy in self.sent:
+            copy.wait_send()
+
+    def cols(self, j):
+        return pl.ds(j * self.width, self.width)
+
+    def shard(self, index, j):
+        return self.a_ref.at[pl.ds(pl.multiple_of(index * self.rows, self.rows), self.rows), self.cols(j)]
+
+    def slots(self):
+        return (self.nz - 1) + (self.ny - 1) * self.nz + self.nz * self.ny
+
+    def pass_on(self, what, number, index, j, peer):
+        ref = self.shard(index, j)
+        self.send((what, number, j), j * self.slots() + number, ref, ref, peer)
+
+    def sibling(self):
+        return self.index(self.z, self.y, 1 - self.c)
+
+    def gather_start(self):
+        self.a_ref[pl.ds(pl.multiple_of(self.me * self.rows, self.rows), self.rows), :] = self.x_ref[...]
+        for j in range(CHUNKS):
+            for d in range(1, self.nz):
+                self.pass_on("g", d - 1, self.me, j, self.index(self.zp(d), self.y, self.c))
+            self.spread(0, j)
+
+    def spread(self, dz, j):
+        index = self.index(self.zm(dz), self.y, self.c)
+        for dy in range(1, self.ny):
+            self.pass_on("g", (self.nz - 1) + (dy - 1) * self.nz + dz, index, j, self.index(self.z, self.yp(dy), self.c))
+        self.pass_on("g", (self.nz - 1) + (self.ny - 1) * self.nz + dz, index, j, self.sibling())
+
+    def gather_z(self, j):
+        for dz in range(1, self.nz):
+            self.arrived(("g", dz - 1, j))
+            self.spread(dz, j)
+
+    def gather_y(self, j):
+        base = (self.nz - 1) + (self.ny - 1) * self.nz
+        for dy in range(1, self.ny):
+            for dz in range(self.nz):
+                self.arrived(("g", (self.nz - 1) + (dy - 1) * self.nz + dz, j))
+                index = self.index(self.zm(dz), self.ym(dy), self.c)
+                self.pass_on("g", base + dy * self.nz + dz, index, j, self.sibling())
+
+    def gather_done(self, j):
+        base = (self.nz - 1) + (self.ny - 1) * self.nz
+        for n in range(self.nz * self.ny):
+            self.arrived(("g", base + n, j))
+
+    def number(self, j, slot):
+        return CHUNKS * self.slots() + j * (1 + (self.ny - 1) + (self.nz - 1)) + slot
+
+    def reduce_core(self, j):
+        cols = self.cols(j)
+        self.send(("c", j), self.number(j, 0), self.da_ref.at[:, 1 - self.c, :, cols],
+                  self.rc.at[:, :, cols], self.sibling())
+
+    def reduce_y(self, j):
+        cols = self.cols(j)
+        self.arrived(("c", j))
+        for dy in range(self.ny):
+            y = self.yp(dy)
+            for z in range(self.nz):
+                chip = z * self.ny + y
+                total = self.da_ref[chip, self.c, :, cols] + self.rc[chip, :, cols]
+                if dy == 0:
+                    self.keep[z, :, cols] = total
+                else:
+                    self.sy[dy - 1, z, :, cols] = total
+            if dy > 0:
+                self.send(("y", dy, j), self.number(j, dy), self.sy.at[dy - 1, :, :, cols],
+                          self.ry.at[dy - 1, :, :, cols], self.index(self.z, y, self.c))
+
+    def reduce_z(self, j):
+        cols = self.cols(j)
+        for dy in range(1, self.ny):
+            self.arrived(("y", dy, j))
+        for dz in [*range(1, self.nz), 0]:
+            z = self.zp(dz)
+            total = self.keep[z, :, cols]
+            for dy in range(1, self.ny):
+                total = total + self.ry[dy - 1, z, :, cols]
+            if dz == 0:
+                self.out_ref[:, cols] = total
+            else:
+                self.sz[dz - 1, :, cols] = total
+                self.send(("z", dz, j), self.number(j, self.ny - 1 + dz), self.sz.at[dz - 1, :, cols],
+                          self.rz.at[dz - 1, :, cols], self.index(z, self.y, self.c))
+
+    def reduce_done(self, j):
+        cols = self.cols(j)
+        total = self.out_ref[:, cols]
+        for dz in range(1, self.nz):
+            self.arrived(("z", dz, j))
+            total = total + self.rz[dz - 1, :, cols]
+        self.out_ref[:, cols] = total
+
+
+def kernel(H, W, parts, linked, x_ref, y_ref, logit_ref, p_ref, out_ref,
+           wc, wr, re_ref, lam, rq1, rq2, rq3, rb2, rb3, u, p1, p2, acc, usum, *rest):
+    if linked:
+        a_ref, da_ref = rest[:2]
+        links = Links(parts, H // parts, x_ref, out_ref, a_ref, da_ref, *rest[2:8], rest[8:10])
+        links.barrier()
+        links.gather_start()
+
+        def get_da(c):
+            return da_ref[:, :, :, c].reshape(H, W)
+
+        def set_da(c, value):
+            da_ref[:, :, :, c] = value.reshape(parts // 2, 2, H // parts, W)
+    else:
+        a_ref = x_ref
+
+        def get_da(c):
+            return out_ref[:, c]
+
+        def set_da(c, value):
+            out_ref[:, c] = value
+
     gc = kernel_matrix(W)
     gr = kernel_matrix(H)
     ch, cl = split(gc)
@@ -67,11 +246,14 @@
         out = out[:H] + out[H:]
         return [out[:, n * W:(n + 1) * W] for n in range(len(fields))]
 
-    def over_slabs(step):
+    def over_slabs(step, begin=0, end=K):
         def one(s, carry):
             step([pl.ds(pl.multiple_of((s * SLAB + n) * W, W), W) for n in range(SLAB)])
             return carry
-        lax.fori_loop(0, K // SLAB, one, 0)
+        lax.fori_loop(begin // SLAB, end // SLAB, one, 0)
+
+    def over_chunk(step, j):
+        over_slabs(step, j * K // CHUNKS, (j + 1) * K // CHUNKS)
 
     def add(total, parts):
         s = parts[0]
@@ -86,7 +268,17 @@
         for c, x in zip(cols, q):
             rq1[:, c] = 1.0 / x
         add(acc, [lam[:, c] * jnp.log(x) for c, x in zip(cols, q)])
-    over_slabs(first)
+    if linked:
+        for t in range(CHUNKS + 2):
+            if t < CHUNKS:
+                links.gather_z(t)
+            if 0 <= t - 1 < CHUNKS:
+                links.gather_y(t - 1)
+            if t >= 2:
+                links.gather_done(t - 2)
+                over_chunk(first, t - 2)
+    else:
+        over_slabs(first)
 
     def forward(p, rq_in, rb, rq_out):
         p[...] = jnp.exp(acc[...])
@@ -126,10 +318,7 @@
             for c, x in zip(cols, dr):
                 inv = rb[:, c]
                 t = x * inv
-                if newest:
-                    da_ref[:, c] = t
-                else:
-                    da_ref[:, c] += t
+                set_da(c, t if newest else get_da(c) + t)
                 db.append(t * (a_ref[:, c] * inv))
             dv = blur(db)
             parts = []
@@ -147,31 +336,69 @@
     def last(cols):
         d = blur([(u[:, c] - lam[:, c] * usum[...]) * rq1[:, c] for c in cols])
         for c, x in zip(cols, d):
-            da_ref[:, c] += x * re_ref[...]
-    over_slabs(last)
+            set_da(c, get_da(c) + x * re_ref[...])
+    if linked:
+        for t in range(CHUNKS + 3):
+            if t < CHUNKS:
+                over_chunk(last, t)
+                links.reduce_core(t)
+            if 0 <= t - 1 < CHUNKS:
+                links.reduce_y(t - 1)
+            if 0 <= t - 2 < CHUNKS:
+                links.reduce_z(t - 2)
+            if t >= 3:
+                links.reduce_done(t - 3)
+        links.finish()
+    else:
+        over_slabs(last)
 
 
 def body(atoms, images, logits, *, parts):
     rows, wide = atoms.shape
     H, W = rows * parts, wide // K
-    gathered = lax.all_gather(atoms, "atom", axis=0, tiled=True)
+    linked = rows % 8 == 0 and images.shape[0] == 1 and parts % 2 == 0
     field = pltpu.VMEM((H, wide), f32)
     plane = pltpu.VMEM((H, W), f32)
+    scratch = [
+        pltpu.VMEM((2 * W, 2 * W), bf16),
+        pltpu.VMEM((2 * H, 2 * H), bf16),
+        plane,
+        pltpu.VMEM((1, wide), f32),
+        field, field, field, field, field, field,
+        plane, plane, plane, plane,
+    ]
+    extra = {}
+    if linked:
+        nz, ny = chip_grid(parts)
+        copies = CHUNKS * ((nz - 1) + (ny - 1) * nz + nz * ny + 1 + (ny - 1) + (nz - 1))
+        scratch += [
+            field,
+            pltpu.VMEM((nz * ny, 2, rows, wide), f32),
+            pltpu.VMEM((nz * ny, rows, wide), f32),
+            pltpu.VMEM((max(ny - 1, 1), nz, rows, wide), f32),
+            pltpu.VMEM((max(ny - 1, 1), nz, rows, wide), f32),
+            pltpu.VMEM((nz, rows, wide), f32),
+            pltpu.VMEM((max(nz - 1, 1), rows, wide), f32),
+            pltpu.VMEM((max(nz - 1, 1), rows, wide), f32),
+            pltpu.SemaphoreType.DMA((copies,)),
+            pltpu.SemaphoreType.DMA((copies,)),
+        ]
+        extra = dict(collective_id=0, has_side_effects=True)
     call = pl.pallas_call(
-        functools.partial(kernel, H, W),
-        out_shape=(jax.ShapeDtypeStruct((H, W), f32), jax.ShapeDtypeStruct((H, wide), f32)),
+        functools.partial(kernel, H, W, parts, linked),
+        out_shape=(
+            jax.ShapeDtypeStruct((H, W), f32),
+            jax.ShapeDtypeStruct((rows if linked else H, wide), f32),
+        ),
         in_specs=[pl.BlockSpec(memory_space=pltpu.VMEM)] * 3,
         out_specs=[pl.BlockSpec(memory_space=pltpu.VMEM)] * 2,
-        scratch_shapes=[
-            pltpu.VMEM((2 * W, 2 * W), bf16),
-            pltpu.VMEM((2 * H, 2 * H), bf16),
-            plane,
-            pltpu.VMEM((1, wide), f32),
-            field, field, field, field, field, field,
-            plane, plane, plane, plane,
-        ],
-        compiler_params=pltpu.CompilerParams(vmem_limit_bytes=40 * 2**20),
+        scratch_shapes=scratch,
+        compiler_params=pltpu.CompilerParams(vmem_limit_bytes=44 * 2**20, **extra),
     )
+    if linked:
+        p, da = call(atoms, images.reshape(H, W), logits)
+        return p.reshape(1, H * W), da
+    gathered = lax.all_gather(atoms, "atom", axis=0, tiled=True)
     results, grads = [], []
     for n in range(images.shape[0]):
         p, da = call(gathered, images[n].reshape(H, W), logits[n:n + 1])

time: 162 us -> 79.8 us (0.49)
  waiting for transfers between devices: 108 us -> 0 us
  Pallas kernels: 37.5 us -> 75.3 us
  between operations: 14 us -> 0.65 us
    reduce_scatter x1 -> x0, waiting for transfers between devices: 60.5 us -> none  [body(): lax.psum_scatter(term, 'atom', scatter_dimension=0, tiled=True)]
    all_gather x1 -> x0, waiting for transfers between devices: 46.3 us -> none  [body(): gathered = lax.all_gather(atoms, 'atom', axis=0, tiled=True)]
    pallas_call x1, Pallas kernels: 37.5 us -> 75.3 us  [body(): p, da = call(atoms, images.reshape(H, W), logits)]
    unnamed x6 -> x8, local copies, waits for them, and re-layouts: 3.08 us -> 3.68 us
  transfers between devices with their start and end apart: 2 -> 0, of which waited for: 2 -> 0; matrix products, arithmetic and copies ran while one was open for 0% -> 0% of each run, Pallas kernels for 0% -> 0%
where the time goes in v1:
time: 79.8 us; the launch traced here: 79.6 us
  Pallas kernels  75.3 us (94%)
  local copies, waits for them, and re-layouts  3.68 us (5%)
    pallas_call x1, Pallas kernels, body(): p, da = call(atoms, images.reshape(H, W), logits)  75.3 us
    unnamed x8, local copies, waits for them, and re-layouts  3.68 us

profile of v1, /device:TPU:0, one launch (start us, length us, event | category | flops | bytes accessed | tf_op | source)
XLA Modules:
  0.0 79.6 jit_solution(53734586651641491)
XLA Ops:
  0.6 0.0 copy-start.2
  0.6 0.6 copy-done.2
  1.3 0.0 copy-start
  1.3 0.9 %copy-done = f32[8,4096]{1,0:T(8,128)S(1)} copy-done((f32[8,4096]{1,0:T(8,128)S(1)}, f32[8,4096]{1,0:T(8,128)}, u32[]{:S(2)}) %copy-start) | copy-done | bytes 131096
  2.2 0.0 copy-start.1
  2.2 0.8 %copy-done.1 = f32[1,16384]{1,0:T(1,128)S(1)} copy-done((f32[1,16384]{1,0:T(1,128)S(1)}, f32[1,16384]{1,0:T(1,128)}, u32[]{:S(2)}) %copy-start.1) | copy-done | bytes 65560
  3.0 75.3 %shard_map.50 = (f32[128,128]{1,0:T(8,128)S(1)}, f32[8,4096]{1,0:T(8,128)S(1)}) custom-call(f32[8,4096]{1,0:T(8,128)S(1)} %copy-done, f32[128,128]{1,0:T(8,128)S(1)} %bitcast.2, f32[1,32]{1,0:T(1,128)S(1)} %copy-done.2), custom_call_target="tpu_custom_call" | custom-call | tf_op jit(solution)/shard_map/pallas_call | solution.py:399
  78.3 0.6 copy.7
  79.0 0.7 copy.8
Async XLA Ops:
  0.6 0.7 copy-start.2
  1.3 0.9 %copy-start = (f32[8,4096]{1,0:T(8,128)S(1)}, f32[8,4096]{1,0:T(8,128)}, u32[]{:S(2)}) copy-start(f32[8,4096]{1,0:T(8,128)} %x_ref.1) | copy-start | bytes 393220
  2.2 0.8 %copy-start.1 = (f32[1,16384]{1,0:T(1,128)S(1)}, f32[1,16384]{1,0:T(1,128)}, u32[]{:S(2)}) copy-start(f32[1,16384]{1,0:T(1,128)} %param.4) | copy-start | bytes 196612

commit v2 on v1

--- a/solution.py
+++ b/solution.py
@@ -11,8 +11,8 @@
 K = 32
 HALF = 15
 SPREAD = 50.0
-SLAB = 4
-CHUNKS = 4
+SLAB = 16
+CHUNKS = 2
 
 f32 = jnp.float32
 bf16 = jnp.bfloat16

time: 79.8 us -> 64.3 us (0.81)
  Pallas kernels: 75.3 us -> 59.8 us
    pallas_call x1, Pallas kernels: 75.3 us -> 59.8 us  [body(): p, da = call(atoms, images.reshape(H, W), logits)]
where the time goes in v2:
time: 64.3 us; the launch traced here: 64.1 us
  Pallas kernels  59.8 us (93%)
  local copies, waits for them, and re-layouts  3.68 us (6%)
  between operations  0.65 us (1%)
    pallas_call x1, Pallas kernels, body(): p, da = call(atoms, images.reshape(H, W), logits)  59.8 us
    unnamed x8, local copies, waits for them, and re-layouts  3.68 us

profile of v2, /device:TPU:0, one launch (start us, length us, event | category | flops | bytes accessed | tf_op | source)
XLA Modules:
  0.0 64.1 jit_solution(17861106316062131990)
XLA Ops:
  0.6 0.0 copy-start.2
  0.6 0.6 %copy-done.2 = f32[1,32]{1,0:T(1,128)S(1)} copy-done((f32[1,32]{1,0:T(1,128)S(1)}, f32[1,32]{1,0:T(1,128)}, u32[]{:S(2)}) %copy-start.2) | copy-done | bytes 152
  1.3 0.0 copy-start
  1.3 0.9 %copy-done = f32[8,4096]{1,0:T(8,128)S(1)} copy-done((f32[8,4096]{1,0:T(8,128)S(1)}, f32[8,4096]{1,0:T(8,128)}, u32[]{:S(2)}) %copy-start) | copy-done | bytes 131096
  2.2 0.0 copy-start.1
  2.2 0.8 %copy-done.1 = f32[1,16384]{1,0:T(1,128)S(1)} copy-done((f32[1,16384]{1,0:T(1,128)S(1)}, f32[1,16384]{1,0:T(1,128)}, u32[]{:S(2)}) %copy-start.1) | copy-done | bytes 65560
  3.0 59.8 %shard_map.50 = (f32[128,128]{1,0:T(8,128)S(1)}, f32[8,4096]{1,0:T(8,128)S(1)}) custom-call(f32[8,4096]{1,0:T(8,128)S(1)} %copy-done, f32[128,128]{1,0:T(8,128)S(1)} %bitcast.2, f32[1,32]{1,0:T(1,128)S(1)} %copy-done.2), custom_call_target="tpu_custom_call" | custom-call | tf_op jit(solution)/shard_map/pallas_call | solution.py:399
  62.9 0.6 copy.7
  63.5 0.7 %copy.8 = f32[8,4096]{1,0:T(8,128)} copy(f32[8,4096]{1,0:T(8,128)S(1)} %get-tuple-element.9) | data formatting | bytes 262144
Async XLA Ops:
  0.6 0.7 %copy-start.2 = (f32[1,32]{1,0:T(1,128)S(1)}, f32[1,32]{1,0:T(1,128)}, u32[]{:S(2)}) copy-start(f32[1,32]{1,0:T(1,128)} %logit_ref.1) | copy-start | bytes 388
  1.3 0.9 %copy-start = (f32[8,4096]{1,0:T(8,128)S(1)}, f32[8,4096]{1,0:T(8,128)}, u32[]{:S(2)}) copy-start(f32[8,4096]{1,0:T(8,128)} %x_ref.1) | copy-start | bytes 393220
  2.2 0.8 %copy-start.1 = (f32[1,16384]{1,0:T(1,128)S(1)}, f32[1,16384]{1,0:T(1,128)}, u32[]{:S(2)}) copy-start(f32[1,16384]{1,0:T(1,128)} %param.4) | copy-start | bytes 196612

commit v3 on v2

--- a/solution.py
+++ b/solution.py
@@ -250,7 +250,7 @@
         def one(s, carry):
             step([pl.ds(pl.multiple_of((s * SLAB + n) * W, W), W) for n in range(SLAB)])
             return carry
-        lax.fori_loop(begin // SLAB, end // SLAB, one, 0)
+        lax.fori_loop(begin // SLAB, end // SLAB, one, 0, unroll=True)
 
     def over_chunk(step, j):
         over_slabs(step, j * K // CHUNKS, (j + 1) * K // CHUNKS)

time: 64.3 us -> 61.8 us (0.961)
  Pallas kernels: 59.8 us -> 57.3 us
    pallas_call x1, Pallas kernels: 59.8 us -> 57.3 us  [body(): p, da = call(atoms, images.reshape(H, W), logits)]
where the time goes in v3:
time: 61.8 us; the launch traced here: 61.7 us
  Pallas kernels  57.3 us (93%)
  local copies, waits for them, and re-layouts  3.68 us (6%)
  between operations  0.65 us (1%)
    pallas_call x1, Pallas kernels, body(): p, da = call(atoms, images.reshape(H, W), logits)  57.3 us
    unnamed x8, local copies, waits for them, and re-layouts  3.68 us

profile of v3, /device:TPU:0, one launch (start us, length us, event | category | flops | bytes accessed | tf_op | source)
XLA Modules:
  0.0 61.7 jit_solution(8219638501248236226)
XLA Ops:
  0.6 0.0 copy-start.2
  0.6 0.6 %copy-done.2 = f32[1,32]{1,0:T(1,128)S(1)} copy-done((f32[1,32]{1,0:T(1,128)S(1)}, f32[1,32]{1,0:T(1,128)}, u32[]{:S(2)}) %copy-start.2) | copy-done | bytes 152
  1.3 0.0 copy-start
  1.3 0.9 %copy-done = f32[8,4096]{1,0:T(8,128)S(1)} copy-done((f32[8,4096]{1,0:T(8,128)S(1)}, f32[8,4096]{1,0:T(8,128)}, u32[]{:S(2)}) %copy-start) | copy-done | bytes 131096
  2.2 0.0 copy-start.1
  2.2 0.8 %copy-done.1 = f32[1,16384]{1,0:T(1,128)S(1)} copy-done((f32[1,16384]{1,0:T(1,128)S(1)}, f32[1,16384]{1,0:T(1,128)}, u32[]{:S(2)}) %copy-start.1) | copy-done | bytes 65560
  3.0 57.3 %shard_map.50 = (f32[128,128]{1,0:T(8,128)S(1)}, f32[8,4096]{1,0:T(8,128)S(1)}) custom-call(f32[8,4096]{1,0:T(8,128)S(1)} %copy-done, f32[128,128]{1,0:T(8,128)S(1)} %bitcast.2, f32[1,32]{1,0:T(1,128)S(1)} %copy-done.2), custom_call_target="tpu_custom_call" | custom-call | tf_op jit(solution)/shard_map/pallas_call | solution.py:399
  60.4 0.6 %copy.7 = f32[1,16384]{1,0:T(1,128)} copy(f32[1,16384]{1,0:T(1,128)S(1)} %bitcast.3) | data formatting | bytes 131072
  61.0 0.7 %copy.8 = f32[8,4096]{1,0:T(8,128)} copy(f32[8,4096]{1,0:T(8,128)S(1)} %get-tuple-element.9) | data formatting | bytes 262144
Async XLA Ops:
  0.6 0.7 %copy-start.2 = (f32[1,32]{1,0:T(1,128)S(1)}, f32[1,32]{1,0:T(1,128)}, u32[]{:S(2)}) copy-start(f32[1,32]{1,0:T(1,128)} %logit_ref.1) | copy-start | bytes 388
  1.3 0.9 %copy-start = (f32[8,4096]{1,0:T(8,128)S(1)}, f32[8,4096]{1,0:T(8,128)}, u32[]{:S(2)}) copy-start(f32[8,4096]{1,0:T(8,128)} %x_ref.1) | copy-start | bytes 393220
  2.2 0.8 %copy-start.1 = (f32[1,16384]{1,0:T(1,128)S(1)}, f32[1,16384]{1,0:T(1,128)}, u32[]{:S(2)}) copy-start(f32[1,16384]{1,0:T(1,128)} %param.4) | copy-start | bytes 196612
